TPU v7x, 32 devices: a whole 2x2x4 slice. The times are simulated.
32 devices in a mesh: groups: 2 (over y), feat: 4 (over z), dp: 4 (over x, core).
Axes of the slice: x: 2, y: 2, z: 4, core: 2. Of those that a mesh axis runs over, the one named last changes fastest.
Arguments:
- features: bfloat16 [2048, 8192], P(('groups', 'dp'), 'feat'), parts along dimension 0, may hold values from -6 to 6
- bn_gain: float32 [8192], P('feat'), may hold values from 0.1 to 1.9
- bn_shift: float32 [8192], P('feat'), may hold values from -0.5 to 0.5
- weight: bfloat16 [8192, 8192], P('feat'), may hold values from -2 to 2
Outputs:
- covariance: float32 [16384, 8192], P(('groups', 'dp'), 'feat'), parts along dimension 0
- grad_in: bfloat16 [2048, 8192], P(('groups', 'dp'), 'feat'), parts along dimension 0
There are 2 independent parts, one for each index of `groups`. A program takes and returns all parts, laid end to end along the dimension named above; an argument that names none is the same for every part. Nothing has to cross between parts.
All inputs are finite; a program needn't handle non-finite values.
Results may differ from a plain program's by a relative error of at most 0.014.
Values may be sent and summed in bfloat16 or wider, within the bound.
A program may use at most 256 MiB of HBM per device.

v0:
```python
import jax
import jax.numpy as jnp
from jax import lax
from jax.sharding import PartitionSpec as P


def shards(features, bn_gain, bn_shift, weight):
    dp_count = lax.axis_size("dp")
    feat_count = lax.axis_size("feat")
    local_rows = features.shape[0]
    images = local_rows * dp_count
    hidden = features.astype(jnp.float32)
    col_sums, col_squares = lax.psum((jnp.sum(hidden, 0), jnp.sum(hidden * hidden, 0)), "dp")
    mean_h = col_sums / images
    var_h = col_squares / images - mean_h * mean_h
    normed = (hidden - mean_h) * lax.rsqrt(var_h + 1e-05) * bn_gain + bn_shift
    activated = jnp.maximum(normed, 0.0).astype(jnp.bfloat16)
    partial_value = jnp.dot(activated, weight, preferred_element_type=jnp.float32).astype(
        jnp.bfloat16
    )
    proj_f = lax.psum_scatter(partial_value, "feat", scatter_dimension=1, tiled=True).astype(
        jnp.float32
    )
    proj_mean = lax.psum(jnp.sum(proj_f, 0), "dp") / images
    centered = (proj_f - proj_mean).astype(jnp.bfloat16)
    cent_full = lax.all_gather(centered, "feat", axis=1, tiled=True)
    piece = lax.all_gather(centered, "dp", axis=0, tiled=True)
    cent_x = lax.all_to_all(cent_full, "dp", split_axis=1, concat_axis=0, tiled=True)
    gram = lax.psum(
        lax.dot_general(
            centered, piece, (((1,), (1,)), ((), ())), preferred_element_type=jnp.float32
        ),
        "feat",
    )
    piece_f = piece.astype(jnp.float32)
    proj_var = jnp.sum(piece_f * piece_f, 0) / (images - 1)
    spread = jnp.sqrt(proj_var + 0.0001)
    scale_up = images / (images - 1)
    active = jnp.where(spread < 1.0, 1.0 / spread, 0.0)
    factor = lax.all_gather(
        4.0 * scale_up * proj_var + 25.0 * scale_up * active, "feat", axis=0, tiled=True
    )
    scaled = (cent_full.astype(jnp.float32) * factor).astype(jnp.bfloat16)
    dims = (((1,), (1,)), ((), ()))
    through = lax.dot_general(cent_full, weight, dims, preferred_element_type=jnp.float32)
    direct = lax.dot_general(scaled, weight, dims, preferred_element_type=jnp.float32)
    through_all = lax.all_gather(through.astype(jnp.bfloat16), "dp", axis=0, tiled=True)
    covariance = lax.dot_general(
        cent_x, piece, (((0,), (0,)), ((), ())), preferred_element_type=jnp.float32
    ) / (images - 1)
    own = lax.axis_index("dp") * local_rows + jnp.arange(local_rows, dtype=jnp.int32)[:, None]
    same = own == jnp.arange(images, dtype=jnp.int32)[None, :]
    gram = gram * (4.0 * scale_up / (images - 1))
    diag = jnp.sum(jnp.where(same, gram, 0.0), 1, keepdims=True)
    rest = jnp.where(same, 0.0, gram).astype(jnp.bfloat16)
    grad_in = (
        jnp.dot(rest, through_all, preferred_element_type=jnp.float32) + diag * through - direct
    )
    return (covariance, grad_in.astype(jnp.bfloat16))


def solution(mesh):
    in_specs = (P(("groups", "dp"), "feat"), P("feat"), P("feat"), P("feat", None))
    out_specs = (P(("groups", "dp"), "feat"), P(("groups", "dp"), "feat"))
    return jax.shard_map(shards, mesh=mesh, in_specs=in_specs, out_specs=out_specs, check_vma=False)
```

profile of v0, /device:TPU:0, one launch (start us, length us, event | category | flops | bytes accessed | tf_op | source)
XLA Modules:
  0.0 372.7 jit_solution(6901499173663036275)
XLA Ops:
  7.2 0.0 reduce-scatter.2.cloned.1.call-start
  7.2 1.5 convert_reduce_fusion
  8.7 12.7 %all-reduce = (f32[2048]{0:T(1024)S(1)}, f32[2048]{0:T(1024)S(1)}) all-reduce(f32[2048]{0:T(1024)S(1)} %get-tuple-element.3, f32[2048]{0:T(1024)S(1)} %get-tuple-element.2), channel_id=1, replica_groups=mesh['groups'=2,'feat'=4,'dp'=4] {'dp'}, use_global_device_ids=true, to_apply=%region_3.0 | all-reduce | flops 4096 | bytes 32768 | tf_op jit(solution)/shard_map/psum | solution.py:13
  21.4 16.7 %convolution_convert_fusion = bf16[256,8192]{1,0:T(8,128)(2,1)} fusion(bf16[2048,8192]{1,0:T(8,128)(2,1)} %param.7, bf16[256,2048]{1,0:T(8,128)(2,1)} %param.4, f32[2048]{0:T(1024)} %param.6, f32[2048]{0:T(1024)} %param.5, f32[2048]{0:T(1024)S(1)} %get-tuple-element.7, f32[2048]{0:T(1024)S(1)} %get-tuple-element.6), kind=kOutput, calls=%fused_computation | convolution fusion | flops 8595701760 | bytes 38830080 | tf_op jit(solution)/shard_map/dot_general | solution.py:18
  38.1 0.0 reduce-scatter.2.cloned.1.call-update
  38.2 0.0 all-gather.6.cloned.1.call-start
  38.2 77.2 %reduce-scatter.2.cloned.1.call-done = bf16[256,2048]{1,0:T(8,128)(2,1)} async-done(((bf16[256,8192]{1,0:T(8,128)(2,1)}), bf16[256,2048]{1,0:T(8,128)(2,1)}) %reduce-scatter.2.cloned.1.call-update) | async-done | bytes 1048592 | tf_op jit(solution)/shard_map/reduce_scatter | solution.py:21
  115.4 1.4 convert_reduce_fusion.1
  116.8 7.0 %psum.30 = f32[2048]{0:T(1024)S(1)} all-reduce(f32[2048]{0:T(1024)S(1)} %convert_reduce_fusion.1), channel_id=1, replica_groups=mesh['groups'=2,'feat'=4,'dp'=4] {'dp'}, use_global_device_ids=true, to_apply=%region_6.0 | all-reduce | flops 2048 | bytes 16384 | tf_op jit(solution)/shard_map/psum | solution.py:24
  123.8 2.4 fusion.4
  126.3 0.0 all-gather.6.cloned.1.call-update
  126.3 0.0 all-gather.4.cloned.1.call-start
  126.3 0.7 all-gather.4.cloned.1.call-update
  127.0 0.0 all-reduce.3.cloned.1.call-start
  127.1 33.4 %all-gather.6.cloned.1.call-done = bf16[1024,2048]{1,0:T(8,128)(2,1)} async-done(((bf16[256,2048]{1,0:T(8,128)(2,1)}), bf16[1024,2048]{1,0:T(8,128)(2,1)}) %all-gather.6.cloned.1.call-update) | async-done | bytes 4194320 | tf_op jit(solution)/shard_map/all_gather | solution.py:27
  160.5 4.8 %fusion.24 = f32[256,1024]{1,0:T(8,128)} fusion(bf16[256,2048]{1,0:T(8,128)(2,1)} %fusion.4, bf16[1024,2048]{1,0:T(8,128)(2,1)} %all-gather.6.cloned.1.call-done), kind=kOutput, calls=%fused_computation.43 | convolution fusion | flops 1073741824 | bytes 6291456 | tf_op jit(solution)/shard_map/dot_general | solution.py:30
  165.3 0.0 all-reduce.3.cloned.1.call-update
  165.3 0.0 all-gather.8.cloned.1.call-start
  165.4 78.1 %all-gather.4.cloned.1.call-done = bf16[256,8192]{1,0:T(8,128)(2,1)} async-done(((bf16[256,2048]{1,0:T(8,128)(2,1)}), bf16[256,8192]{1,0:T(8,128)(2,1)}) %all-gather.4.cloned.1.call-update) | async-done | bytes 4194320 | tf_op jit(solution)/shard_map/all_gather | solution.py:26
  243.5 16.7 %fusion.23 = (bf16[256,2048]{1,0:T(8,128)(2,1)}, f32[256,2048]{1,0:T(8,128)S(1)}) fusion(bf16[256,8192]{1,0:T(8,128)(2,1)} %all-gather.4.cloned.1.call-done, bf16[2048,8192]{1,0:T(8,128)(2,1)} %param.7), kind=kOutput, calls=%fused_computation.42 | convolution fusion | flops 8590458880 | bytes 40894464 | tf_op jit(solution)/shard_map/dot_general | solution.py:45
  260.2 0.0 all-gather.8.cloned.1.call-update
  260.3 4.8 %copy.10 = bf16[32,4,8,2048]{3,2,0,1:T(8,128)(2,1)} copy(bf16[32,4,8,2048]{3,2,1,0:T(8,128)(2,1)} %bitcast.17) | data formatting | bytes 8388608 | tf_op jit(solution)/shard_map/all_to_all | solution.py:28
  265.1 4.9 %all-to-all-start = ((bf16[256,4,2048]{2,0,1:T(8,128)(2,1)}), bf16[256,4,2048]{2,0,1:T(8,128)(2,1)}, u32[]{:S(2)}, u32[]{:S(2)}) async-start(bf16[256,4,2048]{2,0,1:T(8,128)(2,1)} %bitcast.16), calls=%async_computation.1 | async-start | bytes 8388608 | tf_op jit(solution)/shard_map/all_to_all | solution.py:28
  270.0 3.1 multiply_reduce_fusion
  273.1 13.5 %all_gather.15 = f32[8192]{0:T(1024)S(1)} all-gather(f32[2048]{0:T(1024)S(1)} %multiply_add_fusion), channel_id=1, replica_groups=mesh['groups'=2,'feat'=4,'dp'=4] {'feat'}, dimensions={0}, use_global_device_ids=true | all-gather | bytes 40960 | tf_op jit(solution)/shard_map/all_gather | solution.py:40
  286.6 9.9 %all-reduce.3.cloned.1.call-done = f32[256,1024]{1,0:T(8,128)} async-done(((f32[256,1024]{1,0:T(8,128)}), f32[256,1024]{1,0:T(8,128)}) %all-reduce.3.cloned.1.call-update) | async-done | bytes 1048592 | tf_op jit(solution)/shard_map/psum | solution.py:29
  296.5 1.5 select_reduce_fusion
  298.0 30.3 %all-to-all-done = bf16[256,4,2048]{2,0,1:T(8,128)(2,1)} async-done(((bf16[256,4,2048]{2,0,1:T(8,128)(2,1)}), bf16[256,4,2048]{2,0,1:T(8,128)(2,1)}, u32[]{:S(2)}, u32[]{:S(2)}) %all-to-all-start) | async-done | bytes 4194336 | tf_op jit(solution)/shard_map/all_to_all | solution.py:28
  328.3 15.5 %convolution_multiply_fusion = f32[2048,2048]{1,0:T(8,128)} fusion(bf16[1024,2048]{1,0:T(8,128)(2,1)} %bitcast.1, bf16[1024,2048]{1,0:T(8,128)(2,1)} %all-gather.6.cloned.1.call-done), kind=kOutput, calls=%fused_computation.1 | convolution fusion | flops 8594128896 | bytes 25165824 | tf_op jit(solution)/shard_map/dot_general | solution.py:48
  343.9 0.0 copy-done
  343.9 4.9 %convolution_add_fusion = f32[256,2048]{1,0:T(8,128)} fusion(bf16[1024,2048]{1,0:T(8,128)(2,1)} %all-gather.8.cloned.1.call-done, f32[256,2048]{1,0:T(8,128)S(1)} %get-tuple-element.9, f32[256]{0:T(256)S(1)} %select_reduce_fusion, f32[256,1024]{1,0:T(8,128)S(1)} %copy-done, s32[256]{0:T(256)S(1)} %iota_add_fusion), kind=kOutput, calls=%fused_computation.12 | convolution fusion | flops 1075838976 | bytes 9439232 | tf_op jit(solution)/shard_map/dot_general | solution.py:57
  348.8 17.4 %fusion.3 = bf16[256,2048]{1,0:T(8,128)(2,1)} fusion(f32[256,2048]{1,0:T(8,128)} %convolution_add_fusion, bf16[2048,8192]{1,0:T(8,128)(2,1)} %param.7, bf16[256,8192]{1,0:T(8,128)(2,1)} %all-gather.4.cloned.1.call-done, f32[8192]{0:T(1024)S(1)} %all_gather.15), kind=kOutput, calls=%fused_computation.14 | convolution fusion | flops 8597274624 | bytes 40927232 | tf_op jit(solution)/shard_map/dot_general | solution.py:46
  (6 shorter events, 0.0 us)
Async XLA Ops:
  7.2 108.3 %reduce-scatter.2.cloned.1.call-start = ((), (), s32[]{:S(2)}) async-start(), calls=%async_computation.2 | async-start | bytes 5242880 | tf_op jit(solution)/shard_map/reduce_scatter | solution.py:21
  38.2 122.3 %all-gather.6.cloned.1.call-start = ((), (), s32[]{:S(2)}) async-start(), calls=%async_computation.4 | async-start | bytes 5242880 | tf_op jit(solution)/shard_map/all_gather | solution.py:27
  126.3 117.2 %all-gather.4.cloned.1.call-start = ((), (), s32[]{:S(2)}) async-start(), calls=%async_computation.3 | async-start | bytes 5242880 | tf_op jit(solution)/shard_map/all_gather | solution.py:26
  127.0 169.5 %all-reduce.3.cloned.1.call-start = ((), (), s32[]{:S(2)}) async-start(), calls=%async_computation.5 | async-start | bytes 2097152 | tf_op jit(solution)/shard_map/psum | solution.py:29
  165.3 178.5 %all-gather.8.cloned.1.call-start = ((), (), s32[]{:S(2)}) async-start(), calls=%async_computation.6 | async-start | bytes 5242880 | tf_op jit(solution)/shard_map/all_gather | solution.py:47
  265.1 63.3 %all-to-all-start = ((bf16[256,4,2048]{2,0,1:T(8,128)(2,1)}), bf16[256,4,2048]{2,0,1:T(8,128)(2,1)}, u32[]{:S(2)}, u32[]{:S(2)}) async-start(bf16[256,4,2048]{2,0,1:T(8,128)(2,1)} %bitcast.16), calls=%async_computation.1 | async-start | bytes 8388608 | tf_op jit(solution)/shard_map/all_to_all | solution.py:28
  328.3 15.5 %copy-start = (f32[256,1024]{1,0:T(8,128)S(1)}, f32[256,1024]{1,0:T(8,128)}, u32[]{:S(2)}) copy-start(f32[256,1024]{1,0:T(8,128)} %all-reduce.3.cloned.1.call-done) | copy-start | bytes 3145732
Sparse Core Ops, SparseCore 0:
  38.3 77.0 reduce-scatter.1
  126.4 34.0 all-gather.5
  162.7 80.7 all-gather.3
  245.9 50.6 all-reduce.2
  298.5 43.7 all-gather.7
where the time goes:
time: 373 us
  waiting for transfers between devices  230 us (62%)
  matrix products  76.1 us (20%)
  blocking collectives  33.1 us (9%)
  between operations  13.8 us (4%)
  other arithmetic  9.99 us (3%)
  starting transfers between devices  5.14 us (1%)
  local copies, waits for them, and re-layouts  4.82 us (1%)
    all_gather x1, waiting for transfers between devices, shards(): cent_full = lax.all_gather(centered, 'feat', axis=1, tiled=True)  78.1 us
    reduce_scatter x1, waiting for transfers between devices, shards(): lax.psum_scatter(partial_value, 'feat', scatter_dimension=1, tiled=True)  77.2 us
    all_gather x1, waiting for transfers between devices, shards(): piece = lax.all_gather(centered, 'dp', axis=0, tiled=True)  33.4 us
    all_to_all x1, waiting for transfers between devices, shards(): lax.all_to_all(cent_full, 'dp', split_axis=1, concat_axis=0, tiled=True)  30.3 us
    dot_general x1, matrix products, shards(): lax.dot_general(scaled, weight, dims, preferred_element_type=jnp.float32)  17.4 us
    dot_general x1, matrix products, shards(): lax.dot_general(cent_full, weight, dims, preferred_element_type=jnp.float32)  16.7 us
    dot_general x1, matrix products, shards(): jnp.dot(activated, weight, preferred_element_type=jnp.float32)  16.7 us
    dot_general x1, matrix products, shards(): lax.dot_general(cent_x, piece, (((0,), (0,)), ((), ())), preferred_elemen...  15.5 us
  transfers between devices with their start and end apart: 6, of which 5 were waited for; matrix products, arithmetic and copies ran while one was open for 12% of the time, Pallas kernels for 0%

commit v1 on v0

--- a/solution.py
+++ b/solution.py
@@ -26,11 +26,14 @@
     cent_full = lax.all_gather(centered, "feat", axis=1, tiled=True)
     piece = lax.all_gather(centered, "dp", axis=0, tiled=True)
     cent_x = lax.all_to_all(cent_full, "dp", split_axis=1, concat_axis=0, tiled=True)
-    gram = lax.psum(
-        lax.dot_general(
-            centered, piece, (((1,), (1,)), ((), ())), preferred_element_type=jnp.float32
+    gram = jnp.sum(
+        lax.all_gather(
+            lax.dot_general(
+                centered, piece, (((1,), (1,)), ((), ())), preferred_element_type=jnp.float32
+            ),
+            "feat",
         ),
-        "feat",
+        axis=0,
     )
     piece_f = piece.astype(jnp.float32)
     proj_var = jnp.sum(piece_f * piece_f, 0) / (images - 1)

time: 373 us -> 389 us (1.043)
  waiting for transfers between devices: 230 us -> 243 us
    all_gather x1, waiting for transfers between devices: 0.01 us -> 22.1 us  [shards(): lax.all_gather(through.astype(jnp.bfloat16), 'dp', axis=0, tiled=True)]
    psum x1 -> x0, waiting for transfers between devices: 9.88 us -> none  [shards(): lax.psum(lax.dot_general(centered, piece, (((1,), (1,)), ((), ())), prefe...]
  transfers between devices with their start and end apart: 6 -> 6, of which waited for: 5 -> 5; matrix products, arithmetic and copies ran while one was open for 12% -> 13% of each run, Pallas kernels for 0% -> 0%
where the time goes in v1:
time: 389 us
  waiting for transfers between devices  243 us (62%)
  matrix products  77.2 us (20%)
  blocking collectives  33.1 us (9%)
  between operations  13.8 us (4%)
  other arithmetic  11.5 us (3%)
  starting transfers between devices  5.07 us (1%)
  local copies, waits for them, and re-layouts  4.79 us (1%)
    all_gather x1, waiting for transfers between devices, shards(): cent_full = lax.all_gather(centered, 'feat', axis=1, tiled=True)  78.2 us
    reduce_scatter x1, waiting for transfers between devices, shards(): lax.psum_scatter(partial_value, 'feat', scatter_dimension=1, tiled=True)  77.2 us
    all_gather x1, waiting for transfers between devices, shards(): piece = lax.all_gather(centered, 'dp', axis=0, tiled=True)  33.4 us
    all_to_all x1, waiting for transfers between devices, shards(): lax.all_to_all(cent_full, 'dp', split_axis=1, concat_axis=0, tiled=True)  31.6 us
    all_gather x1, waiting for transfers between devices, shards(): lax.all_gather(through.astype(jnp.bfloat16), 'dp', axis=0, tiled=True)  22.1 us
    dot_general x1, matrix products, shards(): lax.dot_general(scaled, weight, dims, preferred_element_type=jnp.float32)  17.4 us
    dot_general x1, matrix products, shards(): lax.dot_general(cent_full, weight, dims, preferred_element_type=jnp.float32)  17.3 us
    dot_general x1, matrix products, shards(): jnp.dot(activated, weight, preferred_element_type=jnp.float32)  16.7 us
  transfers between devices with their start and end apart: 6, of which 5 were waited for; matrix products, arithmetic and copies ran while one was open for 13% of the time, Pallas kernels for 0%

profile of v1, /device:TPU:0, one launch (start us, length us, event | category | flops | bytes accessed | tf_op | source)
XLA Modules:
  0.0 388.8 jit_solution(5192971002771917382)
XLA Ops:
  7.2 0.0 reduce-scatter.2.cloned.1.call-start
  7.2 1.5 convert_reduce_fusion
  8.7 12.7 %all-reduce = (f32[2048]{0:T(1024)S(1)}, f32[2048]{0:T(1024)S(1)}) all-reduce(f32[2048]{0:T(1024)S(1)} %get-tuple-element.3, f32[2048]{0:T(1024)S(1)} %get-tuple-element.2), channel_id=1, replica_groups=mesh['groups'=2,'feat'=4,'dp'=4] {'dp'}, use_global_device_ids=true, to_apply=%region_3.0 | all-reduce | flops 4096 | bytes 32768 | tf_op jit(solution)/shard_map/psum | solution.py:13
  21.4 16.7 %convolution_convert_fusion = bf16[256,8192]{1,0:T(8,128)(2,1)} fusion(bf16[2048,8192]{1,0:T(8,128)(2,1)} %param.7, bf16[256,2048]{1,0:T(8,128)(2,1)} %param.4, f32[2048]{0:T(1024)} %param.6, f32[2048]{0:T(1024)} %param.5, f32[2048]{0:T(1024)S(1)} %get-tuple-element.7, f32[2048]{0:T(1024)S(1)} %get-tuple-element.6), kind=kOutput, calls=%fused_computation | convolution fusion | flops 8595701760 | bytes 38830080 | tf_op jit(solution)/shard_map/dot_general | solution.py:18
  38.1 0.0 reduce-scatter.2.cloned.1.call-update
  38.2 0.0 all-gather.8.cloned.1.call-start
  38.2 77.2 %reduce-scatter.2.cloned.1.call-done = bf16[256,2048]{1,0:T(8,128)(2,1)} async-done(((bf16[256,8192]{1,0:T(8,128)(2,1)}), bf16[256,2048]{1,0:T(8,128)(2,1)}) %reduce-scatter.2.cloned.1.call-update) | async-done | bytes 1048592 | tf_op jit(solution)/shard_map/reduce_scatter | solution.py:21
  115.4 1.4 convert_reduce_fusion.1
  116.8 7.0 %psum.23 = f32[2048]{0:T(1024)S(1)} all-reduce(f32[2048]{0:T(1024)S(1)} %convert_reduce_fusion.1), channel_id=1, replica_groups=mesh['groups'=2,'feat'=4,'dp'=4] {'dp'}, use_global_device_ids=true, to_apply=%region_6.0 | all-reduce | flops 2048 | bytes 16384 | tf_op jit(solution)/shard_map/psum | solution.py:24
  123.8 2.4 fusion.4
  126.3 0.0 all-gather.8.cloned.1.call-update
  126.3 0.0 all-gather.6.cloned.1.call-start
  126.3 0.7 all-gather.6.cloned.1.call-update
  127.0 0.0 all-gather.12.cloned.1.call-start
  127.1 33.4 %all-gather.8.cloned.1.call-done = bf16[1024,2048]{1,0:T(8,128)(2,1)} async-done(((bf16[256,2048]{1,0:T(8,128)(2,1)}), bf16[1024,2048]{1,0:T(8,128)(2,1)}) %all-gather.8.cloned.1.call-update) | async-done | bytes 4194320 | tf_op jit(solution)/shard_map/all_gather | solution.py:27
  160.5 4.8 %fusion.24 = f32[256,1024]{1,0:T(8,128)} fusion(bf16[256,2048]{1,0:T(8,128)(2,1)} %fusion.4, bf16[1024,2048]{1,0:T(8,128)(2,1)} %all-gather.8.cloned.1.call-done), kind=kOutput, calls=%fused_computation.43 | convolution fusion | flops 1073741824 | bytes 6291456 | tf_op jit(solution)/shard_map/dot_general | solution.py:31
  165.3 0.0 all-gather.12.cloned.1.call-update
  165.3 0.0 all-gather.10.cloned.1.call-start
  165.3 78.2 %all-gather.6.cloned.1.call-done = bf16[256,8192]{1,0:T(8,128)(2,1)} async-done(((bf16[256,2048]{1,0:T(8,128)(2,1)}), bf16[256,8192]{1,0:T(8,128)(2,1)}) %all-gather.6.cloned.1.call-update) | async-done | bytes 4194320 | tf_op jit(solution)/shard_map/all_gather | solution.py:26
  243.5 17.3 %fusion.23 = (bf16[256,2048]{1,0:T(8,128)(2,1)}, f32[256,2048]{1,0:T(8,128)S(1)}) fusion(bf16[256,8192]{1,0:T(8,128)(2,1)} %all-gather.6.cloned.1.call-done, bf16[2048,8192]{1,0:T(8,128)(2,1)} %param.7), kind=kOutput, calls=%fused_computation.42 | convolution fusion | flops 8590458880 | bytes 40894464 | tf_op jit(solution)/shard_map/dot_general | solution.py:48
  260.9 0.0 all-gather.10.cloned.1.call-update
  260.9 4.8 %copy.11 = bf16[32,4,8,2048]{3,2,0,1:T(8,128)(2,1)} copy(bf16[32,4,8,2048]{3,2,1,0:T(8,128)(2,1)} %bitcast.18) | data formatting | bytes 8388608 | tf_op jit(solution)/shard_map/all_to_all | solution.py:28
  265.7 4.9 %all-to-all-start = ((bf16[256,4,2048]{2,0,1:T(8,128)(2,1)}), bf16[256,4,2048]{2,0,1:T(8,128)(2,1)}, u32[]{:S(2)}, u32[]{:S(2)}) async-start(bf16[256,4,2048]{2,0,1:T(8,128)(2,1)} %bitcast.17), calls=%async_computation.1 | async-start | bytes 8388608 | tf_op jit(solution)/shard_map/all_to_all | solution.py:28
  270.6 3.1 multiply_reduce_fusion
  273.7 13.5 %all_gather.23 = f32[8192]{0:T(1024)S(1)} all-gather(f32[2048]{0:T(1024)S(1)} %multiply_add_fusion), channel_id=1, replica_groups=mesh['groups'=2,'feat'=4,'dp'=4] {'feat'}, dimensions={0}, use_global_device_ids=true | all-gather | bytes 40960 | tf_op jit(solution)/shard_map/all_gather | solution.py:43
  287.2 31.6 %all-to-all-done = bf16[256,4,2048]{2,0,1:T(8,128)(2,1)} async-done(((bf16[256,4,2048]{2,0,1:T(8,128)(2,1)}), bf16[256,4,2048]{2,0,1:T(8,128)(2,1)}, u32[]{:S(2)}, u32[]{:S(2)}) %all-to-all-start) | async-done | bytes 4194336 | tf_op jit(solution)/shard_map/all_to_all | solution.py:28
  318.8 16.0 %convolution_multiply_fusion = f32[2048,2048]{1,0:T(8,128)} fusion(bf16[1024,2048]{1,0:T(8,128)(2,1)} %bitcast.1, bf16[1024,2048]{1,0:T(8,128)(2,1)} %all-gather.8.cloned.1.call-done), kind=kOutput, calls=%fused_computation.1 | convolution fusion | flops 8594128896 | bytes 25165824 | tf_op jit(solution)/shard_map/dot_general | solution.py:51
  334.8 2.8 reduce_sum.57
  337.6 0.3 select_reduce_fusion
  337.9 22.1 %all-gather.10.cloned.1.call-done = bf16[1024,2048]{1,0:T(8,128)(2,1)} async-done(((bf16[256,2048]{1,0:T(8,128)(2,1)}), bf16[1024,2048]{1,0:T(8,128)(2,1)}) %all-gather.10.cloned.1.call-update) | async-done | bytes 4194320 | tf_op jit(solution)/shard_map/all_gather | solution.py:50
  359.9 4.9 %convolution_add_fusion = f32[256,2048]{1,0:T(8,128)} fusion(bf16[1024,2048]{1,0:T(8,128)(2,1)} %all-gather.10.cloned.1.call-done, f32[256,2048]{1,0:T(8,128)S(1)} %get-tuple-element.9, f32[256]{0:T(256)S(1)} %select_reduce_fusion, f32[256,1024]{1,0:T(8,128)S(1)} %reduce_sum.57, s32[256]{0:T(256)S(1)} %iota_add_fusion), kind=kOutput, calls=%fused_computation.12 | convolution fusion | flops 1075838976 | bytes 9439232 | tf_op jit(solution)/shard_map/dot_general | solution.py:60
  364.9 17.4 %fusion.3 = bf16[256,2048]{1,0:T(8,128)(2,1)} fusion(f32[256,2048]{1,0:T(8,128)} %convolution_add_fusion, bf16[2048,8192]{1,0:T(8,128)(2,1)} %param.7, bf16[256,8192]{1,0:T(8,128)(2,1)} %all-gather.6.cloned.1.call-done, f32[8192]{0:T(1024)S(1)} %all_gather.23), kind=kOutput, calls=%fused_computation.14 | convolution fusion | flops 8597274624 | bytes 40927232 | tf_op jit(solution)/shard_map/dot_general | solution.py:49
  (5 shorter events, 0.0 us)
Async XLA Ops:
  7.2 108.3 %reduce-scatter.2.cloned.1.call-start = ((), (), s32[]{:S(2)}) async-start(), calls=%async_computation.2 | async-start | bytes 5242880 | tf_op jit(solution)/shard_map/reduce_scatter | solution.py:21
  38.2 122.3 %all-gather.8.cloned.1.call-start = ((), (), s32[]{:S(2)}) async-start(), calls=%async_computation.4 | async-start | bytes 5242880 | tf_op jit(solution)/shard_map/all_gather | solution.py:27
  126.3 117.2 %all-gather.6.cloned.1.call-start = ((), (), s32[]{:S(2)}) async-start(), calls=%async_computation.3 | async-start | bytes 5242880 | tf_op jit(solution)/shard_map/all_gather | solution.py:26
  127.0 207.8 %all-gather.12.cloned.1.call-start = ((), (), s32[]{:S(2)}) async-start(), calls=%async_computation.6 | async-start | bytes 5242880 | tf_op jit(solution)/shard_map/all_gather | solution.py:30
  165.3 194.6 %all-gather.10.cloned.1.call-start = ((), (), s32[]{:S(2)}) async-start(), calls=%async_computation.5 | async-start | bytes 5242880 | tf_op jit(solution)/shard_map/all_gather | solution.py:50
  265.7 53.1 %all-to-all-start = ((bf16[256,4,2048]{2,0,1:T(8,128)(2,1)}), bf16[256,4,2048]{2,0,1:T(8,128)(2,1)}, u32[]{:S(2)}, u32[]{:S(2)}) async-start(bf16[256,4,2048]{2,0,1:T(8,128)(2,1)} %bitcast.17), calls=%async_computation.1 | async-start | bytes 8388608 | tf_op jit(solution)/shard_map/all_to_all | solution.py:28
Sparse Core Ops, SparseCore 0:
  38.3 77.0 reduce-scatter.1
  126.4 34.0 all-gather.7
  162.7 80.7 all-gather.5
  245.0 79.7 all-gather.11
  326.8 33.0 all-gather.9
